TPU v7x, 32 devices: a whole 2x2x4 slice. The times are simulated.
32 devices in a mesh: row: 8 (over z, x), col: 4 (over y, core).
Axes of the slice: x: 2, y: 2, z: 4, core: 2. Of those that a mesh axis runs over, the one named last changes fastest.
Arguments:
- gate_pre: bfloat16 [1024, 26624], P('col', 'row'), may hold values from -6 to 6
- up_pre: bfloat16 [1024, 26624], P('col', 'row'), may hold values from -6 to 6
- out_grad: bfloat16 [1024, 8192], P('row', 'col'), may hold values from -0.29882812 to 0.29882812
- w_gate: bfloat16 [8192, 26624], P('col', 'row'), may hold values from -0.0625 to 0.0625
- w_up: bfloat16 [8192, 26624], P('col', 'row'), may hold values from -0.0625 to 0.0625
- w_down: bfloat16 [26624, 8192], P('row', 'col'), may hold values from -1.5 to 1.5
Outputs:
- input_grad: bfloat16 [1024, 8192], P('row', 'col')
- down_wgrad: bfloat16 [26624, 8192], P('row', 'col')
All inputs are finite; a program needn't handle non-finite values.
Results may differ from a plain program's by a relative error of at most 0.012.
Values may be sent and summed in bfloat16 or wider, within the bound.
A program may use at most 192 MiB of HBM per device.

v0:
```python
import jax
import jax.numpy as jnp
from jax import lax
from jax.sharding import PartitionSpec as P


def contract_last(left, right):
    return lax.dot_general(
        left, right, (((1,), (1,)), ((), ())), preferred_element_type=jnp.float32
    )


def contract_first(left, right):
    return lax.dot_general(
        left, right, (((0,), (0,)), ((), ())), preferred_element_type=jnp.float32
    )


def body(gate_pre, up_pre, out_grad, w_gate, w_up, w_down):
    grad_all = lax.all_gather(out_grad, "row", axis=0, tiled=True)
    hidden_sum = lax.psum_scatter(
        contract_last(grad_all, w_down), "col", scatter_dimension=0, tiled=True
    )
    hidden_grad = hidden_sum.astype(jnp.bfloat16).astype(jnp.float32)
    gate_f = gate_pre.astype(jnp.float32)
    up_f = up_pre.astype(jnp.float32)
    sig = jax.nn.sigmoid(gate_f)
    gate_grad = (hidden_grad * up_f * sig * (1.0 + gate_f * (1.0 - sig))).astype(jnp.bfloat16)
    up_grad = (hidden_grad * gate_f * sig).astype(jnp.bfloat16)
    hidden = (gate_f * sig * up_f).astype(jnp.bfloat16)
    gate_all, up_all, hidden_all = (
        lax.all_gather(gate_grad, "col", axis=0, tiled=True),
        lax.all_gather(up_grad, "col", axis=0, tiled=True),
        lax.all_gather(hidden, "col", axis=0, tiled=True),
    )
    input_sum = lax.psum_scatter(
        contract_last(gate_all, w_gate) + contract_last(up_all, w_up),
        "row",
        scatter_dimension=0,
        tiled=True,
    )
    down_sum = contract_first(hidden_all, grad_all)
    return (input_sum.astype(jnp.bfloat16), down_sum.astype(jnp.bfloat16))


def solution(mesh):
    in_specs = (
        P("col", "row"),
        P("col", "row"),
        P("row", "col"),
        P("col", "row"),
        P("col", "row"),
        P("row", "col"),
    )
    out_specs = (P("row", "col"), P("row", "col"))
    return jax.shard_map(body, mesh=mesh, in_specs=in_specs, out_specs=out_specs, check_vma=False)
```

profile of v0, /device:TPU:0, one launch (start us, length us, event | category | flops | bytes accessed | tf_op | source)
XLA Modules:
  0.0 530.7 jit_solution(4760144727811469378)
XLA Ops:
  7.2 0.0 all-gather.5.cloned.1.call-start
  7.2 0.7 all-gather.5.cloned.1.call-update
  7.9 0.0 reduce-scatter.3.cloned.1.call-start
  7.9 78.3 %all-gather.5.cloned.1.call-done = bf16[1024,2048]{1,0:T(8,128)(2,1)} async-done(((bf16[128,2048]{1,0:T(8,128)(2,1)}), bf16[1024,2048]{1,0:T(8,128)(2,1)}) %all-gather.5.cloned.1.call-update) | async-done | bytes 4194320 | tf_op jit(solution)/shard_map/all_gather | solution.py:20
  86.3 22.6 %fusion.10 = f32[1024,3328]{1,0:T(8,128)} fusion(bf16[1024,2048]{1,0:T(8,128)(2,1)} %all-gather.5.cloned.1.call-done, bf16[3328,2048]{1,0:T(8,128)(2,1)} %param.11), kind=kOutput, calls=%fused_computation.18 | convolution fusion | flops 13958643712 | bytes 31457280 | tf_op jit(solution)/shard_map/dot_general | solution.py:8
  108.8 0.0 copy-start
  108.8 0.0 copy-start.1
  108.8 0.0 reduce-scatter.3.cloned.1.call-update
  108.8 0.0 all-gather.7.cloned.1.call-start
  108.9 104.3 %reduce-scatter.3.cloned.1.call-done = f32[256,3328]{1,0:T(8,128)} async-done(((f32[1024,3328]{1,0:T(8,128)}), f32[256,3328]{1,0:T(8,128)}) %reduce-scatter.3.cloned.1.call-update) | async-done | bytes 3407888 | tf_op jit(solution)/shard_map/reduce_scatter | solution.py:21
  213.2 0.0 copy-done
  213.2 0.0 copy-done.1
  213.2 4.9 fusion.9
  218.1 0.0 all-gather.7.cloned.1.call-update
  218.1 0.0 all-gather.9.cloned.1.call-start
  218.1 0.5 all-gather.9.cloned.1.call-update
  218.7 0.0 all-gather.11.cloned.1.call-start
  218.7 0.5 all-gather.11.cloned.1.call-update
  219.3 0.2 reduce-scatter.5.cloned.1.call-start
  219.5 48.1 %all-gather.7.cloned.1.call-done = bf16[1024,3328]{1,0:T(8,128)(2,1)} async-done(((bf16[256,3328]{1,0:T(8,128)(2,1)}), bf16[1024,3328]{1,0:T(8,128)(2,1)}) %all-gather.7.cloned.1.call-update) | async-done | bytes 6815760 | tf_op jit(solution)/shard_map/all_gather | solution.py:32
  267.6 20.2 %fusion.11 = f32[1024,2048]{1,0:T(8,128)} fusion(bf16[1024,3328]{1,0:T(8,128)(2,1)} %all-gather.7.cloned.1.call-done, bf16[2048,3328]{1,0:T(8,128)(2,1)} %param.9), kind=kOutput, calls=%fused_computation.19 | convolution fusion | flops 13958643712 | bytes 28835840 | tf_op jit(solution)/shard_map/dot_general | solution.py:8
  287.8 30.7 %all-gather.9.cloned.1.call-done = bf16[1024,3328]{1,0:T(8,128)(2,1)} async-done(((bf16[256,3328]{1,0:T(8,128)(2,1)}), bf16[1024,3328]{1,0:T(8,128)(2,1)}) %all-gather.9.cloned.1.call-update) | async-done | bytes 6815760 | tf_op jit(solution)/shard_map/all_gather | solution.py:33
  318.4 22.5 %convolution_add_fusion = f32[1024,2048]{1,0:T(8,128)} fusion(f32[1024,2048]{1,0:T(8,128)} %fusion.11, bf16[1024,3328]{1,0:T(8,128)(2,1)} %all-gather.9.cloned.1.call-done, bf16[2048,3328]{1,0:T(8,128)(2,1)} %param.10), kind=kOutput, calls=%fused_computation.5 | convolution fusion | flops 13960740864 | bytes 37224448 | tf_op jit(solution)/shard_map/dot_general | solution.py:8
  340.9 0.0 reduce-scatter.5.cloned.1.call-update
  340.9 28.3 %all-gather.11.cloned.1.call-done = bf16[1024,3328]{1,0:T(8,128)(2,1)} async-done(((bf16[256,3328]{1,0:T(8,128)(2,1)}), bf16[1024,3328]{1,0:T(8,128)(2,1)}) %all-gather.11.cloned.1.call-update) | async-done | bytes 6815760 | tf_op jit(solution)/shard_map/all_gather | solution.py:34
  369.2 20.7 %convolution_convert_fusion = bf16[3328,2048]{1,0:T(8,128)(2,1)} fusion(bf16[1024,3328]{1,0:T(8,128)(2,1)} %all-gather.11.cloned.1.call-done, bf16[1024,2048]{1,0:T(8,128)(2,1)} %all-gather.5.cloned.1.call-done), kind=kOutput, calls=%fused_computation | convolution fusion | flops 13965459456 | bytes 24641536 | tf_op jit(solution)/shard_map/dot_general | solution.py:14
  389.9 131.8 %reduce-scatter.5.cloned.1.call-done = f32[128,2048]{1,0:T(8,128)} async-done(((f32[1024,2048]{1,0:T(8,128)}), f32[128,2048]{1,0:T(8,128)}) %reduce-scatter.5.cloned.1.call-update) | async-done | bytes 1048592 | tf_op jit(solution)/shard_map/reduce_scatter | solution.py:36
  521.7 2.1 convert_element_type.33
Async XLA Ops:
  7.2 79.1 %all-gather.5.cloned.1.call-start = ((), (), s32[]{:S(2)}) async-start(), calls=%async_computation.2 | async-start | bytes 4718592 | tf_op jit(solution)/shard_map/all_gather | solution.py:20
  7.9 205.3 %reduce-scatter.3.cloned.1.call-start = ((), (), s32[]{:S(2)}) async-start(), calls=%async_computation.3 | async-start | bytes 17039360 | tf_op jit(solution)/shard_map/reduce_scatter | solution.py:21
  108.8 104.4 %copy-start = (bf16[256,3328]{1,0:T(8,128)(2,1)S(1)}, bf16[256,3328]{1,0:T(8,128)(2,1)}, u32[]{:S(2)}) copy-start(bf16[256,3328]{1,0:T(8,128)(2,1)} %param.6) | copy-start | bytes 5111812
  108.8 104.4 %copy-start.1 = (bf16[256,3328]{1,0:T(8,128)(2,1)S(1)}, bf16[256,3328]{1,0:T(8,128)(2,1)}, u32[]{:S(2)}) copy-start(bf16[256,3328]{1,0:T(8,128)(2,1)} %param.7) | copy-start | bytes 5111812
  108.8 158.8 %all-gather.7.cloned.1.call-start = ((), (), s32[]{:S(2)}) async-start(), calls=%async_computation.4 | async-start | bytes 8519680 | tf_op jit(solution)/shard_map/all_gather | solution.py:32
  218.1 100.3 %all-gather.9.cloned.1.call-start = ((), (), s32[]{:S(2)}) async-start(), calls=%async_computation.5 | async-start | bytes 8519680 | tf_op jit(solution)/shard_map/all_gather | solution.py:33
  218.7 150.6 %all-gather.11.cloned.1.call-start = ((), (), s32[]{:S(2)}) async-start(), calls=%async_computation.7 | async-start | bytes 8519680 | tf_op jit(solution)/shard_map/all_gather | solution.py:34
  219.3 302.5 %reduce-scatter.5.cloned.1.call-start = ((), (), s32[]{:S(2)}) async-start(), calls=%async_computation.6 | async-start | bytes 9437184 | tf_op jit(solution)/shard_map/reduce_scatter | solution.py:36
Sparse Core Ops, SparseCore 0:
  10.1 76.0 all-gather.4
  109.0 104.2 reduce-scatter.2
  218.2 49.3 all-gather.6
  269.0 49.3 all-gather.8
  319.8 49.3 all-gather.10
  372.7 148.9 reduce-scatter.4
where the time goes:
time: 531 us
  waiting for transfers between devices  423 us (80%)
  matrix products  85.9 us (16%)
  between operations  14.1 us (3%)
  other arithmetic  6.94 us (1%)
    reduce_scatter x1, waiting for transfers between devices, body(): lax.psum_scatter(contract_last(gate_all, w_gate) + contract_last(up_all,...  132 us
    reduce_scatter x1, waiting for transfers between devices, body(): lax.psum_scatter(contract_last(grad_all, w_down), 'col', scatter_dimensio...  104 us
    all_gather x1, waiting for transfers between devices, body(): grad_all = lax.all_gather(out_grad, 'row', axis=0, tiled=True)  78.3 us
    dot_general x3, matrix products, contract_last(): lax.dot_general(left, right, (((1,), (1,)), ((), ())), preferred_element_...  65.2 us
    all_gather x1, waiting for transfers between devices, body(): lax.all_gather(gate_grad, 'col', axis=0, tiled=True)  48.1 us
    all_gather x1, waiting for transfers between devices, body(): lax.all_gather(up_grad, 'col', axis=0, tiled=True)  30.7 us
    all_gather x1, waiting for transfers between devices, body(): lax.all_gather(hidden, 'col', axis=0, tiled=True)  28.3 us
    dot_general x1, matrix products, contract_first(): lax.dot_general(left, right, (((0,), (0,)), ((), ())), preferred_element_...  20.7 us
  transfers between devices with their start and end apart: 6, of which 6 were waited for; matrix products, arithmetic and copies ran while one was open for 12% of the time, Pallas kernels for 0%

commit v1 on v0

v1 whole, which is shorter than its diff:
```python
import functools

import jax
import jax.numpy as jnp
from jax import lax
from jax.sharding import PartitionSpec as P

CHUNKS = 2


def contract_last(left, right):
    return lax.dot_general(
        left, right, (((1,), (1,)), ((), ())), preferred_element_type=jnp.float32
    )


def contract_first(left, right):
    return lax.dot_general(
        left, right, (((0,), (0,)), ((), ())), preferred_element_type=jnp.float32
    )


def in_order(parts, mine):
    count = len(parts)
    if count == 2:
        first = mine == 0
        return jnp.stack([jnp.where(first, parts[0], parts[1]),
                          jnp.where(first, parts[1], parts[0])])
    turned = jnp.stack([parts[-place % count] for place in range(2 * count)])
    return lax.dynamic_slice_in_dim(turned, (count - mine) % count, count, 0)


def body(cols, lines, gate_pre, up_pre, out_grad, w_gate, w_up, w_down):
    chips = cols // 2
    minors = max(m for m in (1, 2, 4, 8, 16) if m * m <= lines and lines % m == 0)
    majors = lines // minors
    col, row = lax.axis_index("col"), lax.axis_index("row")
    chip, core = col // 2, col % 2
    major, minor = row // minors, row % minors
    units = gate_pre.shape[1]
    tokens, features = out_grad.shape
    step = tokens // CHUNKS
    all_rows = lines * step
    rows = all_rows // cols

    def other_core(block):
        return lax.ppermute(block, "col", [(i, i ^ 1) for i in range(cols)])

    def other_chip(block, hop):
        return lax.ppermute(
            block, "col", [(i, (i // 2 + hop) % chips * 2 + i % 2) for i in range(cols)]
        )

    def along_major(block, hop):
        return lax.ppermute(
            block, "row",
            [(i, (i // minors + hop) % majors * minors + i % minors) for i in range(lines)],
        )

    def along_minor(block, hop):
        return lax.ppermute(
            block, "row",
            [(i, i // minors * minors + (i + hop) % minors) for i in range(lines)],
        )

    def both_cores(mine):
        theirs = other_core(mine)
        first = core == 0
        even = jnp.where(first, mine, theirs)
        odd = jnp.where(first, theirs, mine)
        return jnp.stack([even, odd], axis=1).reshape(all_rows, units)

    majors_grad = [out_grad] + [along_major(out_grad, hop) for hop in range(1, majors)]
    lines_grad = [
        in_order([block] + [along_minor(block, hop) for hop in range(1, minors)], minor)
        for block in majors_grad
    ]
    grads = in_order(lines_grad, major).reshape(lines, CHUNKS, step, features)
    pre = [
        in_order([block] + [other_chip(block, hop) for hop in range(1, chips)], chip)
        .reshape(chips, lines // cols, CHUNKS, step, units)
        for block in (gate_pre, up_pre)
    ]

    inputs, hiddens, grad_chunks = [], [], []
    for i in range(CHUNKS):
        gate_f, up_f = (
            block[:, :, i].reshape(chips, rows, units).astype(jnp.float32) for block in pre
        )
        grad_chunk = grads[:, i].reshape(all_rows, features)
        grad_chunks.append(grad_chunk)
        part = contract_last(grad_chunk, w_down).astype(jnp.bfloat16)
        part = part.reshape(chips, 2, rows, units)
        first = core == 0
        keep = jnp.where(first, part[:, 0], part[:, 1])
        send = jnp.where(first, part[:, 1], part[:, 0])
        pair = (keep.astype(jnp.float32) + other_core(send).astype(jnp.float32)).astype(jnp.bfloat16)
        total = pair.astype(jnp.float32)
        for hop in range(1, chips):
            total = total + other_chip(pair, hop).astype(jnp.float32)
        hidden_grad = total.astype(jnp.bfloat16).astype(jnp.float32)
        sig = jax.nn.sigmoid(gate_f)
        gate_grad = (hidden_grad * up_f * sig * (1.0 + gate_f * (1.0 - sig))).astype(jnp.bfloat16)
        up_grad = (hidden_grad * gate_f * sig).astype(jnp.bfloat16)
        hiddens.append(both_cores((gate_f * sig * up_f).astype(jnp.bfloat16)))
        gate_all, up_all = both_cores(gate_grad), both_cores(up_grad)
        share = contract_last(gate_all, w_gate) + contract_last(up_all, w_up)
        share = share.astype(jnp.bfloat16).reshape(majors, minors, step, features)

        def for_minor(hop):
            at = (minor + hop) % minors
            return lax.dynamic_slice_in_dim(share, at, 1, 1)[:, 0]

        line = for_minor(0).astype(jnp.float32)
        for hop in range(1, minors):
            line = line + along_minor(for_minor(hop), hop).astype(jnp.float32)

        def for_major(hop):
            at = (major + hop) % majors
            return lax.dynamic_slice_in_dim(line, at, 1, 0)[0]

        result = for_major(0)
        for hop in range(1, majors):
            sent = along_major(for_major(hop).astype(jnp.bfloat16), hop)
            result = result + sent.astype(jnp.float32)
        inputs.append(result.astype(jnp.bfloat16))
    down = contract_first(jnp.concatenate(hiddens), jnp.concatenate(grad_chunks))
    return (jnp.concatenate(inputs), down.astype(jnp.bfloat16))


def solution(mesh):
    in_specs = (
        P("col", "row"),
        P("col", "row"),
        P("row", "col"),
        P("col", "row"),
        P("col", "row"),
        P("row", "col"),
    )
    out_specs = (P("row", "col"), P("row", "col"))
    return jax.shard_map(
        functools.partial(body, mesh.shape["col"], mesh.shape["row"]),
        mesh=mesh, in_specs=in_specs, out_specs=out_specs, check_vma=False,
    )
```

time: 531 us -> 328 us (0.62)
  waiting for transfers between devices: 423 us -> 164 us
  other arithmetic: 6.94 us -> 36.4 us
  starting transfers between devices: 0.42 us -> 24.9 us
  between operations: 14.1 us -> 1.51 us
  local copies, waits for them, and re-layouts: 0.01 us -> 10.2 us
    reduce_scatter x2 -> x0, waiting for transfers between devices: 236 us -> none  [the longest x1 132 us: body(): lax.psum_scatter(contract_last(gate_all, w_gate) + contract_last(up_all,...]
    all_gather x4 -> x0, waiting for transfers between devices: 185 us -> none  [the longest x1 78.3 us: body(): grad_all = lax.all_gather(out_grad, 'row', axis=0, tiled=True)]
    ppermute x0 -> x27, waiting for transfers between devices: none -> 164 us  [the longest x9 72 us: along_major(): lax.ppermute(block, 'row', [(i, (i // minors + hop) % majors * minors + i...]
    ppermute x0 -> x27, starting transfers between devices: none -> 24.9 us  [the longest x9 9.74 us: along_major(): lax.ppermute(block, 'row', [(i, (i // minors + hop) % majors * minors + i...]
    another operation x0 -> x19, other arithmetic: none -> 15.4 us  [the longest x12 11 us: both_cores(): return jnp.stack([even, odd], axis=1).reshape(all_rows, units)]
    convert_element_type x1 -> x5, other arithmetic: 2.08 us -> 8.59 us  [the longest x1 4.46 us: body(): (hidden_grad * up_f * sig * (1.0 + gate_f * (1.0 - sig))).astype(jnp.bflo...]
    dot_general x3 -> x6, matrix products: 65.2 us -> 69 us  [contract_last(): lax.dot_general(left, right, (((1,), (1,)), ((), ())), preferred_element_...]
  transfers between devices with their start and end apart: 6 -> 27, of which waited for: 6 -> 10; matrix products, arithmetic and copies ran while one was open for 12% -> 41% of each run, Pallas kernels for 0% -> 0%
where the time goes in v1:
time: 328 us; the launch traced here: 326 us
  waiting for transfers between devices  164 us (50%)
  matrix products  89.3 us (27%)
  other arithmetic  36.4 us (11%)
  starting transfers between devices  24.9 us (8%)
  local copies, waits for them, and re-layouts  10.2 us (3%)
    ppermute x9, waiting for transfers between devices, along_major(): lax.ppermute(block, 'row', [(i, (i // minors + hop) % majors * minors + i...  72 us
    dot_general x6, matrix products, contract_last(): lax.dot_general(left, right, (((1,), (1,)), ((), ())), preferred_element_...  69 us
    ppermute x4, waiting for transfers between devices, other_chip(): lax.ppermute(block, 'col', [(i, (i // 2 + hop) % chips * 2 + i % 2) for i...  65.4 us
    ppermute x6, waiting for transfers between devices, along_minor(): lax.ppermute(block, 'row', [(i, i // minors * minors + (i + hop) % minors...  26.1 us
    dot_general x1, matrix products, contract_first(): lax.dot_general(left, right, (((0,), (0,)), ((), ())), preferred_element_...  20.3 us
    another operation x12, other arithmetic, both_cores(): return jnp.stack([even, odd], axis=1).reshape(all_rows, units)  11 us
    ppermute x9, starting transfers between devices, along_major(): lax.ppermute(block, 'row', [(i, (i // minors + hop) % majors * minors + i...  9.74 us
    ppermute x6, starting transfers between devices, along_minor(): lax.ppermute(block, 'row', [(i, i // minors * minors + (i + hop) % minors...  7.66 us
  transfers between devices with their start and end apart: 27, of which 10 were waited for; matrix products, arithmetic and copies ran while one was open for 41% of the time, Pallas kernels for 0%

profile of v1, /device:TPU:0, one launch (start us, length us, event | category | flops | bytes accessed | tf_op | source)
XLA Modules:
  0.0 325.8 jit_solution(2560299463255103724)
XLA Ops:
  0.6 3.0 collective-permute-start
  3.6 3.6 %collective-permute-start.1 = (bf16[128,2048]{1,0:T(8,128)(2,1)}, bf16[128,2048]{1,0:T(8,128)(2,1)S(1)}, u32[]{:S(2)}, u32[]{:S(2)}) collective-permute-start(bf16[128,2048]{1,0:T(8,128)(2,1)} %param.8), channel_id=1, source_target_pairs={{0,24},{4,28},{8,0},{12,4},{16,8},{20,12},{24,16},{28,20},{1,25},{... | collective-permute-start | bytes 1572872 | tf_op jit(solution)/shard_map/ppermute | solution.py:55
  7.2 1.0 collective-permute-start.5
  8.2 1.5 collective-permute-start.10
  9.8 6.0 %collective-permute-done = bf16[128,2048]{1,0:T(8,128)(2,1)S(1)} collective-permute-done((bf16[128,2048]{1,0:T(8,128)(2,1)}, bf16[128,2048]{1,0:T(8,128)(2,1)S(1)}, u32[]{:S(2)}, u32[]{:S(2)}) %collective-permute-start) | collective-permute-done | bytes 524320 | tf_op jit(solution)/shard_map/ppermute | solution.py:61
  15.8 1.8 collective-permute-start.9
  17.5 2.4 collective-permute-done.1
  20.0 0.5 collective-permute-start.2
  20.5 31.4 %collective-permute-done.3 = bf16[128,2048]{1,0:T(8,128)(2,1)S(1)} collective-permute-done((bf16[128,2048]{1,0:T(8,128)(2,1)}, bf16[128,2048]{1,0:T(8,128)(2,1)S(1)}, u32[]{:S(2)}, u32[]{:S(2)}) %collective-permute-start.3) | collective-permute-done | bytes 524320 | tf_op jit(solution)/shard_map/ppermute | solution.py:55
  51.9 0.5 collective-permute-start.4
  52.5 1.1 select_bitcast_fusion.21
  53.7 1.6 collective-permute-start.6
  55.3 11.5 %collective-permute-done.4 = bf16[128,2048]{1,0:T(8,128)(2,1)S(1)} collective-permute-done((bf16[128,2048]{1,0:T(8,128)(2,1)S(1)}, bf16[128,2048]{1,0:T(8,128)(2,1)S(1)}, u32[]{:S(2)}, u32[]{:S(2)}) %collective-permute-start.4) | collective-permute-done | bytes 524320 | tf_op jit(solution)/shard_map/ppermute | solution.py:61
  67.0 8.6 %collective-permute-done.6 = bf16[128,2048]{1,0:T(8,128)(2,1)S(1)} collective-permute-done((bf16[128,2048]{1,0:T(8,128)(2,1)S(1)}, bf16[128,2048]{1,0:T(8,128)(2,1)S(1)}, u32[]{:S(2)}, u32[]{:S(2)}) %collective-permute-start.6) | collective-permute-done | bytes 524320 | tf_op jit(solution)/shard_map/ppermute | solution.py:61
  76.1 0.6 constant_dynamic-slice_fusion
  76.7 1.8 fusion.51
  78.5 12.3 %convolution_convert_fusion.1 = bf16[512,3328]{1,0:T(8,128)(2,1)S(1)} fusion(bf16[512,2048]{1,0:T(8,128)(2,1)} %bitcast.218, bf16[3328,2048]{1,0:T(8,128)(2,1)} %param.11), kind=kOutput, calls=%fused_computation.4 | convolution fusion | flops 6981025792 | bytes 19136512 | tf_op jit(solution)/shard_map/dot_general | solution.py:12
  90.8 1.5 select_bitcast_fusion.8
  92.4 0.8 copy-done
  93.1 11.0 %convolution_convert_fusion.2 = bf16[512,3328]{1,0:T(8,128)(2,1)S(1)} fusion(bf16[512,2048]{1,0:T(8,128)(2,1)S(1)} %bitcast.216, bf16[3328,2048]{1,0:T(8,128)(2,1)} %param.11), kind=kOutput, calls=%fused_computation.5 | convolution fusion | flops 6981025792 | bytes 19136512 | tf_op jit(solution)/shard_map/dot_general | solution.py:12
  104.3 0.6 collective-permute-start.7
  104.9 0.7 copy-done.6
  105.6 0.5 copy-done.7
  106.1 2.6 broadcast_select_fusion.1
  108.6 0.4 copy-done.1
  109.1 2.1 fusion.26
  111.1 1.6 collective-permute-start.18
  112.7 1.5 fusion.28
  114.2 1.8 fusion.27
  116.0 0.5 collective-permute-start.8
  116.5 1.5 fusion.29
  118.0 33.1 %collective-permute-done.18 = bf16[2,128,3328]{2,1,0:T(8,128)(2,1)S(1)} collective-permute-done((bf16[2,128,3328]{2,1,0:T(8,128)(2,1)S(1)}, bf16[2,128,3328]{2,1,0:T(8,128)(2,1)S(1)}, u32[]{:S(2)}, u32[]{:S(2)}) %collective-permute-start.18) | collective-permute-done | bytes 1703968 | tf_op jit(solution)/shard_map/ppermute | solution.py:50
  151.2 3.5 %fusion.25 = (bf16[2,128,3328]{2,1,0:T(8,128)(2,1)S(1)}, bf16[2,128,3328]{2,1,0:T(8,128)(2,1)}, bf16[2,128,3328]{2,1,0:T(8,128)(2,1)S(1)}) fusion(bf16[2,2,1,64,3328]{4,3,2,1,0:T(8,128)(2,1)S(1)} %get-tuple-element.21, bf16[2,128,3328]{2,1,0:T(8,128)(2,1)S(1)} %collective-permute-done.18, bf16[2,128,3328]{2,1,0:T(8,128)(2,1)S(1)} %fusion.26, ...), kind=kLoop, calls=%fused_computation.42 | loop fusion | flops 19595264 | bytes 11927552 | tf_op jit(solution)/shard_map/convert_element_type | solution.py:104
  154.7 0.5 collective-permute-start.20
  155.2 32.3 %collective-permute-done.8 = bf16[2,128,3328]{2,1,0:T(8,128)(2,1)} collective-permute-done((bf16[2,128,3328]{2,1,0:T(8,128)(2,1)}, bf16[2,128,3328]{2,1,0:T(8,128)(2,1)}, u32[]{:S(2)}, u32[]{:S(2)}) %collective-permute-start.8) | collective-permute-done | bytes 1703968 | tf_op jit(solution)/shard_map/ppermute | solution.py:50
  187.4 4.5 %fusion.8 = (bf16[2,128,3328]{2,1,0:T(8,128)(2,1)S(1)}, bf16[2,128,3328]{2,1,0:T(8,128)(2,1)S(1)}, bf16[2,128,3328]{2,1,0:T(8,128)(2,1)S(1)}) fusion(bf16[2,2,1,64,3328]{4,3,2,1,0:T(8,128)(2,1)} %get-tuple-element.20, bf16[2,2,1,64,3328]{4,3,2,1,0:T(8,128)(2,1)} %get-tuple-element.16, bf16[2,128,3328]{2,1,0:T(8,128)(2,1)} %collective-permute-done.8, ...), kind=kLoop, calls=%fused_computation.25 | loop fusion | flops 19595264 | bytes 11927552 | tf_op jit(solution)/shard_map/convert_element_type | solution.py:103
  192.0 0.5 collective-permute-start.11
  192.6 0.4 collective-permute-start.25
  193.0 2.2 select_bitcast_fusion.7
  196.5 11.7 %fusion.53 = f32[512,2048]{1,0:T(8,128)} fusion(bf16[512,3328]{1,0:T(8,128)(2,1)S(1)} %bitcast.207, bf16[2048,3328]{1,0:T(8,128)(2,1)} %param.9), kind=kOutput, calls=%fused_computation.134 | convolution fusion | flops 6979321856 | bytes 21233664 | tf_op jit(solution)/shard_map/dot_general | solution.py:12
  208.2 11.0 %add_convert_fusion = bf16[512,2048]{1,0:T(8,128)(2,1)S(1)} fusion(f32[512,2048]{1,0:T(8,128)} %fusion.53, bf16[512,3328]{1,0:T(8,128)(2,1)S(1)} %bitcast.209, bf16[2048,3328]{1,0:T(8,128)(2,1)} %param.10), kind=kOutput, calls=%fused_computation.21 | convolution fusion | flops 6981419008 | bytes 23330816 | tf_op jit(solution)/shard_map/dot_general | solution.py:12
  219.3 1.3 dynamic-slice_bitcast_fusion
  220.5 0.5 collective-permute-start.21
  221.1 1.7 select_bitcast_fusion.10
  222.8 0.3 pad_maximum_fusion.1
  223.3 11.7 %fusion.52 = f32[512,2048]{1,0:T(8,128)} fusion(bf16[512,3328]{1,0:T(8,128)(2,1)S(1)} %bitcast.211, bf16[2048,3328]{1,0:T(8,128)(2,1)} %param.10), kind=kOutput, calls=%fused_computation.133 | convolution fusion | flops 6979321856 | bytes 21233664 | tf_op jit(solution)/shard_map/dot_general | solution.py:12
  235.0 1.7 select_bitcast_fusion.12
  236.7 0.3 pad_maximum_fusion
  237.0 11.3 %add_convert_fusion.1 = bf16[512,2048]{1,0:T(8,128)(2,1)S(1)} fusion(f32[512,2048]{1,0:T(8,128)} %fusion.52, bf16[512,3328]{1,0:T(8,128)(2,1)S(1)} %bitcast.210, bf16[2048,3328]{1,0:T(8,128)(2,1)} %param.9), kind=kOutput, calls=%fused_computation.22 | convolution fusion | flops 6981419008 | bytes 23330816 | tf_op jit(solution)/shard_map/dot_general | solution.py:12
  248.3 1.2 dynamic-slice_bitcast_fusion.1
  249.5 1.5 collective-permute-start.13
  251.0 1.7 select_bitcast_fusion.1
  253.3 1.7 select_bitcast_fusion.3
  255.3 1.9 copy.30
  257.2 20.3 %convolution_convert_fusion = bf16[3328,2048]{1,0:T(8,128)(2,1)} fusion(bf16[512,3328]{1,0:T(8,128)(2,1)S(1)} %bitcast.206, bf16[512,3328]{1,0:T(8,128)(2,1)} %bitcast.208, bf16[512,2048]{1,0:T(8,128)(2,1)} %bitcast.219, bf16[512,2048]{1,0:T(8,128)(2,1)} %bitcast.217), kind=kOutput, calls=%fused_computation | convolution fusion | flops 13987479552 | bytes 24641536 | tf_op jit(solution)/shard_map/dot_general | solution.py:18
  277.5 1.7 convert_add_fusion.2
  279.5 1.9 collective-permute-start.22
  281.4 1.6 convert_add_fusion.3
  283.1 2.4 collective-permute-start.16
  285.5 0.6 collective-permute-start.15
  286.2 3.7 %collective-permute-done.24 = bf16[64,2048]{1,0:T(8,128)(2,1)S(1)} collective-permute-done((bf16[64,2048]{1,0:T(8,128)(2,1)S(1)}, bf16[64,2048]{1,0:T(8,128)(2,1)S(1)}, u32[]{:S(2)}, u32[]{:S(2)}) %collective-permute-start.24) | collective-permute-done | bytes 262176 | tf_op jit(solution)/shard_map/ppermute | solution.py:55
  289.9 14.7 %collective-permute-done.23 = bf16[64,2048]{1,0:T(8,128)(2,1)S(1)} collective-permute-done((bf16[64,2048]{1,0:T(8,128)(2,1)S(1)}, bf16[64,2048]{1,0:T(8,128)(2,1)S(1)}, u32[]{:S(2)}, u32[]{:S(2)}) %collective-permute-start.23) | collective-permute-done | bytes 262176 | tf_op jit(solution)/shard_map/ppermute | solution.py:55
  304.7 19.7 %collective-permute-done.15 = bf16[64,2048]{1,0:T(8,128)(2,1)S(1)} collective-permute-done((bf16[64,2048]{1,0:T(8,128)(2,1)S(1)}, bf16[64,2048]{1,0:T(8,128)(2,1)S(1)}, u32[]{:S(2)}, u32[]{:S(2)}) %collective-permute-start.15) | collective-permute-done | bytes 262176 | tf_op jit(solution)/shard_map/ppermute | solution.py:55
  324.5 0.8 pad_maximum_fusion.8
  (62 shorter events, 4.2 us)
Async XLA Ops:
  0.6 15.1 %collective-permute-start = (bf16[128,2048]{1,0:T(8,128)(2,1)}, bf16[128,2048]{1,0:T(8,128)(2,1)S(1)}, u32[]{:S(2)}, u32[]{:S(2)}) collective-permute-start(bf16[128,2048]{1,0:T(8,128)(2,1)} %param.8), channel_id=1, source_target_pairs={{0,4},{4,0},{8,12},{12,8},{16,20},{20,16},{24,28},{28,24},{1,5},{5... | collective-permute-start | bytes 1572872 | tf_op jit(solution)/shard_map/ppermute | solution.py:61
  3.6 16.3 %collective-permute-start.1 = (bf16[128,2048]{1,0:T(8,128)(2,1)}, bf16[128,2048]{1,0:T(8,128)(2,1)S(1)}, u32[]{:S(2)}, u32[]{:S(2)}) collective-permute-start(bf16[128,2048]{1,0:T(8,128)(2,1)} %param.8), channel_id=1, source_target_pairs={{0,24},{4,28},{8,0},{12,4},{16,8},{20,12},{24,16},{28,20},{1,25},{... | collective-permute-start | bytes 1572872 | tf_op jit(solution)/shard_map/ppermute | solution.py:55
  7.2 44.7 %collective-permute-start.3 = (bf16[128,2048]{1,0:T(8,128)(2,1)}, bf16[128,2048]{1,0:T(8,128)(2,1)S(1)}, u32[]{:S(2)}, u32[]{:S(2)}) collective-permute-start(bf16[128,2048]{1,0:T(8,128)(2,1)} %param.8), channel_id=1, source_target_pairs={{0,16},{4,20},{8,24},{12,28},{16,0},{20,4},{24,8},{28,12},{1,17},{... | collective-permute-start | bytes 1572872 | tf_op jit(solution)/shard_map/ppermute | solution.py:55
  7.2 46.4 %collective-permute-start.5 = (bf16[128,2048]{1,0:T(8,128)(2,1)}, bf16[128,2048]{1,0:T(8,128)(2,1)S(1)}, u32[]{:S(2)}, u32[]{:S(2)}) collective-permute-start(bf16[128,2048]{1,0:T(8,128)(2,1)} %param.8), channel_id=1, source_target_pairs={{0,8},{4,12},{8,16},{12,20},{16,24},{20,28},{24,0},{28,4},{1,9},{5... | collective-permute-start | bytes 1572872 | tf_op jit(solution)/shard_map/ppermute | solution.py:55
  8.2 96.6 %collective-permute-start.10 = (bf16[256,3328]{1,0:T(8,128)(2,1)}, bf16[256,3328]{1,0:T(8,128)(2,1)}, u32[]{:S(2)}, u32[]{:S(2)}) collective-permute-start(bf16[256,3328]{1,0:T(8,128)(2,1)} %param.6), channel_id=1, source_target_pairs={{0,2},{1,3},{2,0},{3,1},{4,6},{5,7},{6,4},{7,5},{8,10},{9,11},{10,... | collective-permute-start | bytes 5111816 | tf_op jit(solution)/shard_map/ppermute | solution.py:50
  15.8 89.1 %collective-permute-start.9 = (bf16[256,3328]{1,0:T(8,128)(2,1)}, bf16[256,3328]{1,0:T(8,128)(2,1)}, u32[]{:S(2)}, u32[]{:S(2)}) collective-permute-start(bf16[256,3328]{1,0:T(8,128)(2,1)} %param.7), channel_id=1, source_target_pairs={{0,2},{1,3},{2,0},{3,1},{4,6},{5,7},{6,4},{7,5},{8,10},{9,11},{10,... | collective-permute-start | bytes 5111816 | tf_op jit(solution)/shard_map/ppermute | solution.py:50
  20.0 35.3 %collective-permute-start.2 = (bf16[128,2048]{1,0:T(8,128)(2,1)S(1)}, bf16[128,2048]{1,0:T(8,128)(2,1)S(1)}, u32[]{:S(2)}, u32[]{:S(2)}) collective-permute-start(bf16[128,2048]{1,0:T(8,128)(2,1)S(1)} %collective-permute-done.1), channel_id=1, source_target_pairs={{0,4},{4,0},{8,12},{12,8},{16,20},{20,16},{24,28},{28,24},{1,5},{5... | collective-permute-start | bytes 1572872 | tf_op jit(solution)/shard_map/ppermute | solution.py:61
  51.9 14.9 %collective-permute-start.4 = (bf16[128,2048]{1,0:T(8,128)(2,1)S(1)}, bf16[128,2048]{1,0:T(8,128)(2,1)S(1)}, u32[]{:S(2)}, u32[]{:S(2)}) collective-permute-start(bf16[128,2048]{1,0:T(8,128)(2,1)S(1)} %collective-permute-done.3), channel_id=1, source_target_pairs={{0,4},{4,0},{8,12},{12,8},{16,20},{20,16},{24,28},{28,24},{1,5},{5... | collective-permute-start | bytes 1572872 | tf_op jit(solution)/shard_map/ppermute | solution.py:61
  53.7 22.0 %collective-permute-start.6 = (bf16[128,2048]{1,0:T(8,128)(2,1)S(1)}, bf16[128,2048]{1,0:T(8,128)(2,1)S(1)}, u32[]{:S(2)}, u32[]{:S(2)}) collective-permute-start(bf16[128,2048]{1,0:T(8,128)(2,1)S(1)} %collective-permute-done.5), channel_id=1, source_target_pairs={{0,4},{4,0},{8,12},{12,8},{16,20},{20,16},{24,28},{28,24},{1,5},{5... | collective-permute-start | bytes 1572872 | tf_op jit(solution)/shard_map/ppermute | solution.py:61
  78.5 14.6 %copy-start.5 = (bf16[8,1,64,2048]{3,2,1,0:T(8,128)(2,1)}, bf16[8,1,64,2048]{3,2,1,0:T(8,128)(2,1)S(1)}, u32[]{:S(2)}) copy-start(bf16[8,1,64,2048]{3,2,1,0:T(8,128)(2,1)S(1)} %get-tuple-element.6) | copy-start | bytes 6291460
  90.8 2.3 copy-start
  93.1 15.5 %collective-permute-start.17 = (bf16[2,128,3328]{2,1,0:T(8,128)(2,1)}, bf16[2,128,3328]{2,1,0:T(8,128)(2,1)}, u32[]{:S(2)}, u32[]{:S(2)}) collective-permute-start(bf16[2,128,3328]{2,1,0:T(8,128)(2,1)} %select_bitcast_fusion.8), channel_id=1, source_target_pairs={{0,1},{1,0},{2,3},{3,2},{4,5},{5,4},{6,7},{7,6},{8,9},{9,8},{10,11... | collective-permute-start | bytes 5111816 | tf_op jit(solution)/shard_map/ppermute | solution.py:47
  104.1 1.5 copy-start.6
  104.1 2.0 copy-start.7
  104.3 9.9 %collective-permute-start.7 = (bf16[2,128,3328]{2,1,0:T(8,128)(2,1)S(1)}, bf16[2,128,3328]{2,1,0:T(8,128)(2,1)S(1)}, u32[]{:S(2)}, u32[]{:S(2)}) collective-permute-start(bf16[2,128,3328]{2,1,0:T(8,128)(2,1)S(1)} %select_bitcast_fusion.13), channel_id=1, source_target_pairs={{0,1},{1,0},{2,3},{3,2},{4,5},{5,4},{6,7},{7,6},{8,9},{9,8},{10,11... | collective-permute-start | bytes 5111816 | tf_op jit(solution)/shard_map/ppermute | solution.py:47
  106.1 3.0 copy-start.1
  111.1 40.1 %collective-permute-start.18 = (bf16[2,128,3328]{2,1,0:T(8,128)(2,1)S(1)}, bf16[2,128,3328]{2,1,0:T(8,128)(2,1)S(1)}, u32[]{:S(2)}, u32[]{:S(2)}) collective-permute-start(bf16[2,128,3328]{2,1,0:T(8,128)(2,1)S(1)} %fusion.26), channel_id=1, source_target_pairs={{0,2},{1,3},{2,0},{3,1},{4,6},{5,7},{6,4},{7,5},{8,10},{9,11},{10,... | collective-permute-start | bytes 5111816 | tf_op jit(solution)/shard_map/ppermute | solution.py:50
  116.0 71.4 %collective-permute-start.8 = (bf16[2,128,3328]{2,1,0:T(8,128)(2,1)}, bf16[2,128,3328]{2,1,0:T(8,128)(2,1)}, u32[]{:S(2)}, u32[]{:S(2)}) collective-permute-start(bf16[2,128,3328]{2,1,0:T(8,128)(2,1)} %fusion.27), channel_id=1, source_target_pairs={{0,2},{1,3},{2,0},{3,1},{4,6},{5,7},{6,4},{7,5},{8,10},{9,11},{10,... | collective-permute-start | bytes 5111816 | tf_op jit(solution)/shard_map/ppermute | solution.py:50
  154.7 37.9 %collective-permute-start.19 = (bf16[2,128,3328]{2,1,0:T(8,128)(2,1)}, bf16[2,128,3328]{2,1,0:T(8,128)(2,1)}, u32[]{:S(2)}, u32[]{:S(2)}) collective-permute-start(bf16[2,128,3328]{2,1,0:T(8,128)(2,1)} %get-tuple-element.5), channel_id=1, source_target_pairs={{0,1},{1,0},{2,3},{3,2},{4,5},{5,4},{6,7},{7,6},{8,9},{9,8},{10,11... | collective-permute-start | bytes 5111816 | tf_op jit(solution)/shard_map/ppermute | solution.py:47
  154.7 41.1 %collective-permute-start.20 = (bf16[2,128,3328]{2,1,0:T(8,128)(2,1)S(1)}, bf16[2,128,3328]{2,1,0:T(8,128)(2,1)S(1)}, u32[]{:S(2)}, u32[]{:S(2)}) collective-permute-start(bf16[2,128,3328]{2,1,0:T(8,128)(2,1)S(1)} %get-tuple-element.4), channel_id=1, source_target_pairs={{0,1},{1,0},{2,3},{3,2},{4,5},{5,4},{6,7},{7,6},{8,9},{9,8},{10,11... | collective-permute-start | bytes 5111816 | tf_op jit(solution)/shard_map/ppermute | solution.py:47
  191.9 29.2 %collective-permute-start.12 = (bf16[2,128,3328]{2,1,0:T(8,128)(2,1)S(1)}, bf16[2,128,3328]{2,1,0:T(8,128)(2,1)}, u32[]{:S(2)}, u32[]{:S(2)}) collective-permute-start(bf16[2,128,3328]{2,1,0:T(8,128)(2,1)S(1)} %get-tuple-element.3), channel_id=1, source_target_pairs={{0,1},{1,0},{2,3},{3,2},{4,5},{5,4},{6,7},{7,6},{8,9},{9,8},{10,11... | collective-permute-start | bytes 5111816 | tf_op jit(solution)/shard_map/ppermute | solution.py:47
  192.0 43.1 %collective-permute-start.11 = (bf16[2,128,3328]{2,1,0:T(8,128)(2,1)S(1)}, bf16[2,128,3328]{2,1,0:T(8,128)(2,1)}, u32[]{:S(2)}, u32[]{:S(2)}) collective-permute-start(bf16[2,128,3328]{2,1,0:T(8,128)(2,1)S(1)} %get-tuple-element.2), channel_id=1, source_target_pairs={{0,1},{1,0},{2,3},{3,2},{4,5},{5,4},{6,7},{7,6},{8,9},{9,8},{10,11... | collective-permute-start | bytes 5111816 | tf_op jit(solution)/shard_map/ppermute | solution.py:47
  192.5 58.5 %collective-permute-start.26 = (bf16[2,128,3328]{2,1,0:T(8,128)(2,1)S(1)}, bf16[2,128,3328]{2,1,0:T(8,128)(2,1)}, u32[]{:S(2)}, u32[]{:S(2)}) collective-permute-start(bf16[2,128,3328]{2,1,0:T(8,128)(2,1)S(1)} %get-tuple-element.8), channel_id=1, source_target_pairs={{0,1},{1,0},{2,3},{3,2},{4,5},{5,4},{6,7},{7,6},{8,9},{9,8},{10,11... | collective-permute-start | bytes 5111816 | tf_op jit(solution)/shard_map/ppermute | solution.py:47
  192.6 60.7 %collective-permute-start.25 = (bf16[2,128,3328]{2,1,0:T(8,128)(2,1)S(1)}, bf16[2,128,3328]{2,1,0:T(8,128)(2,1)}, u32[]{:S(2)}, u32[]{:S(2)}) collective-permute-start(bf16[2,128,3328]{2,1,0:T(8,128)(2,1)S(1)} %get-tuple-element.11), channel_id=1, source_target_pairs={{0,1},{1,0},{2,3},{3,2},{4,5},{5,4},{6,7},{7,6},{8,9},{9,8},{10,11... | collective-permute-start | bytes 5111816 | tf_op jit(solution)/shard_map/ppermute | solution.py:47
  219.3 3.5 %copy-start.2 = (bf16[512,2048]{1,0:T(8,128)(2,1)}, bf16[512,2048]{1,0:T(8,128)(2,1)S(1)}, u32[]{:S(2)}) copy-start(bf16[512,2048]{1,0:T(8,128)(2,1)S(1)} %add_convert_fusion) | copy-start | bytes 6291460
  220.5 56.9 %collective-permute-start.21 = (bf16[4,64,2048]{2,1,0:T(8,128)(2,1)}, bf16[4,64,2048]{2,1,0:T(8,128)(2,1)S(1)}, u32[]{:S(2)}, u32[]{:S(2)}) collective-permute-start(bf16[4,64,2048]{2,1,0:T(8,128)(2,1)} %dynamic-slice_bitcast_fusion), channel_id=1, source_target_pairs={{0,4},{4,0},{8,12},{12,8},{16,20},{20,16},{24,28},{28,24},{1,5},{5... | collective-permute-start | bytes 3145736 | tf_op jit(solution)/shard_map/ppermute | solution.py:61
  248.3 4.4 %copy-start.3 = (bf16[512,2048]{1,0:T(8,128)(2,1)}, bf16[512,2048]{1,0:T(8,128)(2,1)S(1)}, u32[]{:S(2)}) copy-start(bf16[512,2048]{1,0:T(8,128)(2,1)S(1)} %add_convert_fusion.1) | copy-start | bytes 6291460
  249.5 31.9 %collective-permute-start.13 = (bf16[4,64,2048]{2,1,0:T(8,128)(2,1)}, bf16[4,64,2048]{2,1,0:T(8,128)(2,1)}, u32[]{:S(2)}, u32[]{:S(2)}) collective-permute-start(bf16[4,64,2048]{2,1,0:T(8,128)(2,1)} %dynamic-slice_bitcast_fusion.1), channel_id=1, source_target_pairs={{0,4},{4,0},{8,12},{12,8},{16,20},{20,16},{24,28},{28,24},{1,5},{5... | collective-permute-start | bytes 3145736 | tf_op jit(solution)/shard_map/ppermute | solution.py:61
  277.5 3.9 %copy-start.4 = (bf16[512,2048]{1,0:T(8,128)(2,1)S(1)}, bf16[512,2048]{1,0:T(8,128)(2,1)}, u32[]{:S(2)}) copy-start(bf16[512,2048]{1,0:T(8,128)(2,1)} %copy-done.3) | copy-start | bytes 6291460
  279.3 10.6 %collective-permute-start.24 = (bf16[64,2048]{1,0:T(8,128)(2,1)S(1)}, bf16[64,2048]{1,0:T(8,128)(2,1)S(1)}, u32[]{:S(2)}, u32[]{:S(2)}) collective-permute-start(bf16[64,2048]{1,0:T(8,128)(2,1)S(1)} %get-tuple-element.34), channel_id=1, source_target_pairs={{0,24},{4,28},{8,0},{12,4},{16,8},{20,12},{24,16},{28,20},{1,25},{... | collective-permute-start | bytes 786440 | tf_op jit(solution)/shard_map/ppermute | solution.py:55
  279.4 25.2 %collective-permute-start.23 = (bf16[64,2048]{1,0:T(8,128)(2,1)S(1)}, bf16[64,2048]{1,0:T(8,128)(2,1)S(1)}, u32[]{:S(2)}, u32[]{:S(2)}) collective-permute-start(bf16[64,2048]{1,0:T(8,128)(2,1)S(1)} %get-tuple-element.35), channel_id=1, source_target_pairs={{0,16},{4,20},{8,24},{12,28},{16,0},{20,4},{24,8},{28,12},{1,17},{... | collective-permute-start | bytes 786440 | tf_op jit(solution)/shard_map/ppermute | solution.py:55
  279.5 25.1 %collective-permute-start.22 = (bf16[64,2048]{1,0:T(8,128)(2,1)S(1)}, bf16[64,2048]{1,0:T(8,128)(2,1)S(1)}, u32[]{:S(2)}, u32[]{:S(2)}) collective-permute-start(bf16[64,2048]{1,0:T(8,128)(2,1)S(1)} %get-tuple-element.33), channel_id=1, source_target_pairs={{0,8},{4,12},{8,16},{12,20},{16,24},{20,28},{24,0},{28,4},{1,9},{5... | collective-permute-start | bytes 786440 | tf_op jit(solution)/shard_map/ppermute | solution.py:55
  283.1 21.6 %collective-permute-start.16 = (bf16[64,2048]{1,0:T(8,128)(2,1)S(1)}, bf16[64,2048]{1,0:T(8,128)(2,1)S(1)}, u32[]{:S(2)}, u32[]{:S(2)}) collective-permute-start(bf16[64,2048]{1,0:T(8,128)(2,1)S(1)} %get-tuple-element.31), channel_id=1, source_target_pairs={{0,24},{4,28},{8,0},{12,4},{16,8},{20,12},{24,16},{28,20},{1,25},{... | collective-permute-start | bytes 786440 | tf_op jit(solution)/shard_map/ppermute | solution.py:55
  285.5 38.9 %collective-permute-start.15 = (bf16[64,2048]{1,0:T(8,128)(2,1)S(1)}, bf16[64,2048]{1,0:T(8,128)(2,1)S(1)}, u32[]{:S(2)}, u32[]{:S(2)}) collective-permute-start(bf16[64,2048]{1,0:T(8,128)(2,1)S(1)} %get-tuple-element.32), channel_id=1, source_target_pairs={{0,16},{4,20},{8,24},{12,28},{16,0},{20,4},{24,8},{28,12},{1,17},{... | collective-permute-start | bytes 786440 | tf_op jit(solution)/shard_map/ppermute | solution.py:55
  289.9 34.5 %collective-permute-start.14 = (bf16[64,2048]{1,0:T(8,128)(2,1)S(1)}, bf16[64,2048]{1,0:T(8,128)(2,1)S(1)}, u32[]{:S(2)}, u32[]{:S(2)}) collective-permute-start(bf16[64,2048]{1,0:T(8,128)(2,1)S(1)} %get-tuple-element.30), channel_id=1, source_target_pairs={{0,8},{4,12},{8,16},{12,20},{16,24},{20,28},{24,0},{28,4},{1,9},{5... | collective-permute-start | bytes 786440 | tf_op jit(solution)/shard_map/ppermute | solution.py:55
